TPU v7x, 32 devices: a whole 2x2x4 slice. The times are simulated.
32 devices in a mesh: groups: 2 (over y), runs: 4 (over z), sub: 2 (over x), pair: 2 (over core).
Axes of the slice: x: 2, y: 2, z: 4, core: 2. Of those that a mesh axis runs over, the one named last changes fastest.
Arguments:
- embeddings: bfloat16 [8192, 1152], P(('groups', 'runs', 'sub', 'pair')), parts along dimension 0, may hold values from -64 to 64, as said below
- block_cluster: int32 [64], P('groups'), parts along dimension 0, may hold values from 0 to 15, never falling along the last dimension, each value on 1 to 8 neighbouring positions
- owner: int32 [32], P('groups'), parts along dimension 0, may hold values from 0 to 15, each once
Outputs:
- density: float32 [8192], P(('groups', 'runs', 'sub', 'pair')), parts along dimension 0
- prototypes: float32 [32, 1152], P(('groups', 'runs'), 'sub'), parts along dimension 0
There are 2 independent parts, one for each index of `groups`. A program takes and returns all parts, laid end to end along the dimension named above; each array names one. Nothing has to cross between parts.
Inputs may be any that keep to these rules, and one draw needn't show every extreme that they name: `embeddings`: values of order one to a few tens, rows of unlike length. `block_cluster`: never falls along the blocks; each cluster names 1 to 8 consecutive blocks, one exactly 8. `owner`: each slot is named by exactly one cluster.
All inputs are finite; a program needn't handle non-finite values.
Results may differ from a plain program's by a relative error of at most 0.0003.
The roundings to bfloat16 on the way count: a program that leaves them out, or rounds other values in their place, can miss the bound.
Values may be sent and summed in bfloat16 or wider, within the bound.
A program may use at most 64 MiB of HBM per device.

v0:
```python
import jax
import jax.numpy as jnp
from jax import lax
from jax.sharding import PartitionSpec as P

BLOCK = 128


sharpness = 8.0


def from_behind(value, axis, steps):
    count = lax.axis_size(axis)
    initial, last = (max(0, -steps), min(count, count - steps))
    return lax.ppermute(value, axis, [(source, source + steps) for source in range(initial, last)])


def tile_terms(left, right, same):
    width = left.shape[1]
    dots = jnp.einsum("ie,je->ij", left, right, preferred_element_type=jnp.float32)
    return jnp.sum(jnp.where(same, jnp.exp(sharpness * (dots / width) - sharpness), 0.0), axis=1)


def per_device(embeddings, block_cluster, owner):
    rows, width = embeddings.shape
    blk_dev = rows // BLOCK
    n_sub = lax.axis_size("sub")
    n_pair = lax.axis_size("pair")
    n_runs = lax.axis_size("runs")
    blk_run = blk_dev * n_sub * n_pair
    run_pos = lax.axis_index("runs")
    local_pos = lax.axis_index("sub") * n_pair + lax.axis_index("pair")
    values = embeddings.astype(jnp.float32)
    unit = (values * lax.rsqrt(jnp.mean(values * values, axis=-1, keepdims=True) + 1e-06)).astype(
        jnp.bfloat16
    )
    slab = lax.all_gather(unit, ("sub", "pair"), axis=0, tiled=True)
    ids_run = lax.dynamic_slice_in_dim(block_cluster, run_pos * blk_run, blk_run, 0)
    ids_lower = lax.dynamic_slice_in_dim(
        block_cluster, jnp.maximum(run_pos - 1, 0) * blk_run, blk_run, 0
    )
    ids_upper = lax.dynamic_slice_in_dim(
        block_cluster, jnp.minimum(run_pos + 1, n_runs - 1) * blk_run, blk_run, 0
    )
    valid_lower = run_pos > 0
    valid_upper = run_pos < n_runs - 1
    own_ids = lax.dynamic_slice_in_dim(ids_run, local_pos * blk_dev, blk_dev, 0)
    own_rows = jnp.repeat(own_ids, BLOCK)
    slab_rows = jnp.repeat(ids_run, BLOCK)
    density = tile_terms(unit, slab, own_rows[:, None] == slab_rows[None, :])
    lower = from_behind(slab, "runs", 1)
    upper = from_behind(slab, "runs", -1)
    lower_rows = jnp.repeat(ids_lower, BLOCK)
    upper_rows = jnp.repeat(ids_upper, BLOCK)
    density = density + tile_terms(
        unit, lower, (own_rows[:, None] == lower_rows[None, :]) & valid_lower
    )
    density = density + tile_terms(
        unit, upper, (own_rows[:, None] == upper_rows[None, :]) & valid_upper
    )
    weight = 1.0 / density
    block_sum = jnp.einsum(
        "bi,bie->be",
        weight.reshape(blk_dev, BLOCK),
        unit.reshape(blk_dev, BLOCK, width).astype(jnp.float32),
        precision=lax.Precision.HIGHEST,
    )
    block_weight = jnp.sum(weight.reshape(blk_dev, BLOCK), axis=1)
    clusters = owner.shape[0]
    cluster_range = jnp.arange(clusters, dtype=jnp.int32)
    slot = jnp.sum(jnp.where(own_ids[:, None] == cluster_range[None, :], owner[None, :], 0), axis=1)
    place = (slot[:, None] == cluster_range[None, :]).astype(jnp.float32)
    term = jnp.dot(place.T, block_sum, precision=lax.Precision.HIGHEST)
    weight_term = jnp.dot(block_weight, place, precision=lax.Precision.HIGHEST)
    feature_width = width // n_sub
    slot_sum, slot_weight = (
        lax.psum_scatter(term, "runs", scatter_dimension=0, tiled=True),
        lax.psum_scatter(weight_term, "runs", scatter_dimension=0, tiled=True),
    )
    total, weight_total = lax.psum((slot_sum, slot_weight), ("sub", "pair"))
    total = lax.dynamic_slice_in_dim(total, lax.axis_index("sub") * feature_width, feature_width, 1)
    return (density, total / weight_total[:, None])


def solution(mesh):
    placed = (P(("groups", "runs", "sub", "pair"), None), P("groups"), P("groups"))
    return jax.shard_map(
        per_device,
        mesh=mesh,
        in_specs=placed,
        out_specs=(P(("groups", "runs", "sub", "pair")), P(("groups", "runs"), "sub")),
        check_vma=False,
    )
```

profile of v0, /device:TPU:0, one launch (start us, length us, event | category | flops | bytes accessed | tf_op | source)
XLA Modules:
  0.0 152.3 jit_solution(13632673489327603829)
XLA Ops:
  7.2 0.0 copy-start.3
  7.2 0.0 copy-start.1
  7.2 0.0 copy-start.2
  7.2 0.0 all-gather.2.cloned.1.call-start
  7.2 1.3 fusion.12
  8.5 2.1 %fusion.13 = bf16[256,1152]{1,0:T(8,128)(2,1)} fusion(bf16[256,1152]{1,0:T(8,128)(2,1)} %param.3, f32[256]{0:T(256)S(1)} %add_rsqrt_fusion), kind=kLoop, calls=%fused_computation.18 | loop fusion | flops 884736 | bytes 1180672 | tf_op jit(solution)/shard_map/convert_element_type | solution.py:34
  10.6 0.0 all-gather.2.cloned.1.call-update
  10.6 0.0 all-reduce.5.cloned.1.call-start
  10.7 26.9 %all-gather.2.cloned.1.call-done = bf16[1024,1152]{1,0:T(8,128)(2,1)} async-done(((bf16[256,1152]{1,0:T(8,128)(2,1)}), bf16[1024,1152]{1,0:T(8,128)(2,1)}) %all-gather.2.cloned.1.call-update) | async-done | bytes 2359312 | tf_op jit(solution)/shard_map/all_gather | solution.py:37
  37.5 1.3 collective-permute-start.1
  38.8 4.7 %collective-permute-start = (bf16[1024,1152]{1,0:T(8,128)(2,1)}, bf16[1024,1152]{1,0:T(8,128)(2,1)S(1)}, u32[]{:S(2)}, u32[]{:S(2)}) collective-permute-start(bf16[1024,1152]{1,0:T(8,128)(2,1)} %all-gather.2.cloned.1.call-done), channel_id=1, source_target_pairs={{0,4},{4,8},{8,12},{1,5},{5,9},{9,13},{2,6},{6,10},{10,14},{3,7},{... | collective-permute-start | bytes 7077896 | tf_op jit(solution)/shard_map/ppermute | solution.py:15
  43.6 0.0 copy-done.1
  43.6 0.1 dynamic_slice.18
  43.6 0.0 copy-done.3
  43.6 0.6 dynamic-slice
  44.9 0.1 fusion.21
  45.0 0.0 copy-done.2
  45.0 0.2 fusion.17
  45.2 0.1 broadcast_bitcast_fusion.3
  45.2 0.1 broadcast_bitcast_fusion.2
  45.3 0.1 broadcast_bitcast_fusion
  45.4 0.0 copy-start
  45.4 2.9 %fusion.9 = f32[256]{0:T(256)S(1)} fusion(bf16[256,1152]{1,0:T(8,128)(2,1)} %fusion.13, bf16[1024,1152]{1,0:T(8,128)(2,1)} %all-gather.2.cloned.1.call-done, s32[1024]{0:T(1024)S(1)} %broadcast_bitcast_fusion.2, s32[256]{0:T(256)S(1)} %broadcast_bitcast_fusion.3), kind=kOutput, calls=%fused_computation.14 | convolution fusion | flops 605290240 | bytes 2955264 | tf_op jit(solution)/shard_map/ie,je->ij/dot_general | solution.py:20
  48.3 44.8 %collective-permute-done.1 = bf16[1024,1152]{1,0:T(8,128)(2,1)} collective-permute-done((bf16[1024,1152]{1,0:T(8,128)(2,1)}, bf16[1024,1152]{1,0:T(8,128)(2,1)}, u32[]{:S(2)}, u32[]{:S(2)}) %collective-permute-start.1) | collective-permute-done | bytes 2359328 | tf_op jit(solution)/shard_map/ppermute | solution.py:15
  93.1 0.0 copy-done
  93.1 2.7 %fusion.11 = f32[256]{0:T(256)S(1)} fusion(bf16[256,1152]{1,0:T(8,128)(2,1)S(1)} %copy-done, bf16[1024,1152]{1,0:T(8,128)(2,1)} %collective-permute-done.1, s32[1024]{0:T(1024)S(1)} %get-tuple-element.10, s32[256]{0:T(256)S(1)} %broadcast_bitcast_fusion.3, pred[]{:T(512)S(6)} %lt.22), kind=kOutput, calls=%fused_computation.16 | convolution fusion | flops 605552384 | bytes 2955265 | tf_op jit(solution)/shard_map/ie,je->ij/dot_general | solution.py:20
  95.8 0.0 collective-permute-done
  95.9 1.1 fusion.10
  96.9 0.7 bitcast_reduce_fusion
  97.6 0.4 fusion.22
  98.0 0.9 fusion.14
  98.9 0.0 all-reduce.5.cloned.1.call-update
  98.9 0.2 convolution_bitcast_fusion
  99.1 12.4 %all-reduce.1 = f32[16]{0:T(128)S(1)} all-reduce(f32[16]{0:T(128)S(1)} %convolution_bitcast_fusion), channel_id=3, replica_groups=mesh['groups'=2,'runs'=4,'sub'=2,'pair'=2] {'runs'}, use_global_device_ids=true, to_apply=%region_8.9.clone | all-reduce | flops 16 | bytes 128
  111.5 0.1 dynamic-slice.3
  111.6 22.2 %all-reduce.5.cloned.1.call-done = f32[16,1152]{1,0:T(8,128)} async-done(((f32[16,1152]{1,0:T(8,128)}), f32[16,1152]{1,0:T(8,128)}) %all-reduce.5.cloned.1.call-update) | async-done | bytes 73744
  133.8 0.8 constant_dynamic-slice_fusion
  134.5 10.2 %all-reduce.2 = (f32[4,1152]{1,0:T(4,128)S(1)}, f32[4]{0:T(128)S(1)}) all-reduce(f32[4,1152]{1,0:T(4,128)S(1)} %constant_dynamic-slice_fusion, f32[4]{0:T(128)S(1)} %dynamic-slice.3), channel_id=1, replica_groups=mesh['groups'=2,'runs'=4,'sub'=2,'pair'=2] {'sub','pair'}, use_global_device_ids=true, to_apply=%region_6.7 | all-reduce | flops 4612 | bytes 36896 | tf_op jit(solution)/shard_map/psum | solution.py:80
  144.8 0.7 dynamic-slice_divide_fusion
  (1 shorter events, 0.0 us)
Async XLA Ops:
  7.2 36.5 %copy-start.3 = (u32[32]{0:T(128)S(1)}, u32[32]{0:T(128)}, u32[]{:S(2)}) copy-start(u32[32]{0:T(128)} %constant.59) | copy-start | bytes 388
  7.2 36.4 %copy-start.1 = (s32[32]{0:T(128)S(1)}, s32[32]{0:T(128)}, u32[]{:S(2)}) copy-start(s32[32]{0:T(128)} %param.4) | copy-start | bytes 388
  7.2 37.8 %copy-start.2 = (s32[16]{0:T(128)S(1)}, s32[16]{0:T(128)}, u32[]{:S(2)}) copy-start(s32[16]{0:T(128)} %param.5) | copy-start | bytes 196
  7.2 30.3 %all-gather.2.cloned.1.call-start = ((), (), s32[]{:S(2)}) async-start(), calls=%async_computation | async-start | bytes 2949120 | tf_op jit(solution)/shard_map/all_gather | solution.py:37
  10.6 123.2 %all-reduce.5.cloned.1.call-start = ((), (), s32[]{:S(2)}) async-start(), calls=%async_computation.1 | async-start | bytes 147456
  37.5 55.6 %collective-permute-start.1 = (bf16[1024,1152]{1,0:T(8,128)(2,1)}, bf16[1024,1152]{1,0:T(8,128)(2,1)}, u32[]{:S(2)}, u32[]{:S(2)}) collective-permute-start(bf16[1024,1152]{1,0:T(8,128)(2,1)} %all-gather.2.cloned.1.call-done), channel_id=1, source_target_pairs={{4,0},{8,4},{12,8},{5,1},{9,5},{13,9},{6,2},{10,6},{14,10},{7,3},{... | collective-permute-start | bytes 7077896 | tf_op jit(solution)/shard_map/ppermute | solution.py:15
  38.8 57.0 %collective-permute-start = (bf16[1024,1152]{1,0:T(8,128)(2,1)}, bf16[1024,1152]{1,0:T(8,128)(2,1)S(1)}, u32[]{:S(2)}, u32[]{:S(2)}) collective-permute-start(bf16[1024,1152]{1,0:T(8,128)(2,1)} %all-gather.2.cloned.1.call-done), channel_id=1, source_target_pairs={{0,4},{4,8},{8,12},{1,5},{5,9},{9,13},{2,6},{6,10},{10,14},{3,7},{... | collective-permute-start | bytes 7077896 | tf_op jit(solution)/shard_map/ppermute | solution.py:15
  45.4 47.8 %copy-start = (bf16[256,1152]{1,0:T(8,128)(2,1)S(1)}, bf16[256,1152]{1,0:T(8,128)(2,1)}, u32[]{:S(2)}) copy-start(bf16[256,1152]{1,0:T(8,128)(2,1)} %fusion.13) | copy-start | bytes 1769476
Sparse Core Ops, SparseCore 0:
  10.7 26.7 all-gather.1
  99.1 34.6 all-reduce.4
where the time goes:
time: 153 us; the launch traced here: 152 us
  waiting for transfers between devices  93.9 us (61%)
  blocking collectives  22.6 us (15%)
  between operations  14.8 us (10%)
  matrix products  8.21 us (5%)
  starting transfers between devices  6.06 us (4%)
  other arithmetic  4.89 us (3%)
  local copies, waits for them, and re-layouts  1.82 us (1%)
    ppermute x2, waiting for transfers between devices, from_behind(): lax.ppermute(value, axis, [(source, source + steps) for source in range(i...  44.8 us
    all_gather x1, waiting for transfers between devices, per_device(): slab = lax.all_gather(unit, ('sub', 'pair'), axis=0, tiled=True)  26.9 us
    unnamed x3, waiting for transfers between devices  22.2 us
    unnamed x1, blocking collectives  12.4 us
    psum x1, blocking collectives, per_device(): total, weight_total = lax.psum((slot_sum, slot_weight), ('sub', 'pair'))  10.2 us
    dot_general x3, matrix products, tile_terms(): jnp.einsum('ie,je->ij', left, right, preferred_element_type=jnp.float32)  6.74 us
    ppermute x2, starting transfers between devices, from_behind(): lax.ppermute(value, axis, [(source, source + steps) for source in range(i...  5.98 us
  transfers between devices with their start and end apart: 4, of which 3 were waited for; matrix products, arithmetic and copies ran while one was open for 5% of the time, Pallas kernels for 0%

commit v1 on v0

v1 whole, which is shorter than its diff:
```python
import functools

import jax
import jax.numpy as jnp
from jax import lax
from jax.experimental import pallas as pl
from jax.experimental.pallas import tpu as pltpu
from jax.sharding import PartitionSpec as P

BLOCK = 128
SHARPNESS = 8.0
MESH = pl.DeviceIdType.MESH


def kernel(
    sizes,
    x_ref,
    ids_ref,
    owner_ref,
    dens_ref,
    proto_ref,
    slab,
    rx,
    acc,
    ret,
    part,
    msg,
    gathered,
    mate_send,
    mate_recv,
    rows_send,
    rows_recv,
    ret_send,
    part_recv,
    msg_send,
    msg_recv,
):
    n_runs, n_sub, n_pair, blk_dev, lows, lanes, slots = sizes
    rows, width = x_ref.shape
    chips = n_runs * n_sub
    count = chips * n_pair
    blk_chip = blk_dev * n_pair
    run, sub, core = (lax.axis_index(a) for a in ("runs", "sub", "pair"))
    chip = run * n_sub + sub
    me = chip * n_pair + core
    mate = 1 - core

    def at(device_chip, device_core):
        return {
            "runs": device_chip // n_sub,
            "sub": device_chip % n_sub,
            "pair": device_core,
        }

    part[...] = jnp.zeros_like(part)
    acc[...] = jnp.zeros_like(acc)
    ret[...] = jnp.zeros_like(ret)

    barrier = pltpu.get_barrier_semaphore()

    def greet(step, carry):
        other = lax.rem(me + step, count)
        pl.semaphore_signal(
            barrier, inc=1, device_id=at(other // n_pair, other % n_pair), device_id_type=MESH
        )
        return carry

    lax.fori_loop(1, count, greet, 0)

    for b in range(blk_dev):
        span = pl.ds(b * BLOCK, BLOCK)
        values = x_ref[span, :].astype(jnp.float32)
        mean = jnp.sum(values * values, axis=1, keepdims=True) / width
        slab[core, span, :] = (values * lax.rsqrt(mean + 1e-06)).astype(jnp.bfloat16)

    pl.semaphore_wait(barrier, count - 1)

    def target(d):
        return chip + d if d < n_sub else chip - n_sub

    def source(d):
        return chip - d if d < n_sub else chip + n_sub

    def inside(c):
        return (c >= 0) & (c < chips)

    def needed(d, b):
        return (core * blk_dev + b < blk_chip - 1) if d == n_sub else True

    def row_copy(d, b):
        span = pl.ds(b * BLOCK, BLOCK)
        return pltpu.make_async_remote_copy(
            src_ref=slab.at[core, span, :],
            dst_ref=rx.at[d - 1, span, :],
            send_sem=rows_send.at[d - 1, b],
            recv_sem=rows_recv.at[d - 1, b],
            device_id=at(target(d), core),
            device_id_type=MESH,
        )

    steps = [(b, d) for b in range(blk_dev) for d in range(1, n_sub + 1)]
    for b, d in steps:
        @pl.when(inside(target(d)) & needed(d, b))
        def _():
            row_copy(d, b).start()

    mate_copy = pltpu.make_async_remote_copy(
        src_ref=slab.at[core],
        dst_ref=slab.at[core],
        send_sem=mate_send,
        recv_sem=mate_recv,
        device_id=at(chip, mate),
        device_id_type=MESH,
    )
    mate_copy.start()
    mate_arrives = pltpu.make_async_remote_copy(
        src_ref=slab.at[core],
        dst_ref=slab.at[mate],
        send_sem=mate_send,
        recv_sem=mate_recv,
        device_id=at(chip, mate),
        device_id_type=MESH,
    )
    mate_arrives.wait_recv()

    def terms(left, right):
        dots = lax.dot_general(
            left, right, (((1,), (1,)), ((), ())), preferred_element_type=jnp.float32
        )
        return jnp.exp(SHARPNESS * (dots / width) - SHARPNESS)

    def same(left, rights):
        return jnp.concatenate(
            [
                jnp.full((1, BLOCK), jnp.where(ids_ref[r] == ids_ref[left], 1.0, 0.0), jnp.float32)
                for r in rights
            ],
            axis=1,
        )

    own_blocks = [me * blk_dev + b for b in range(blk_dev)]
    chip_blocks = [chip * blk_chip + b for b in range(blk_chip)]

    density = jnp.zeros((1, rows), jnp.float32)
    own = slab[core]
    for j in range(blk_chip):
        c, b = divmod(j, blk_dev)
        t = terms(slab[c, pl.ds(b * BLOCK, BLOCK), :], own)
        density = density + jnp.sum(t, axis=0, keepdims=True) * same(chip_blocks[j], own_blocks)

    def return_copy(d):
        return pltpu.make_async_remote_copy(
            src_ref=ret.at[d - 1],
            dst_ref=part.at[d - 1],
            send_sem=ret_send.at[d - 1],
            recv_sem=part_recv.at[d - 1],
            device_id=at(source(d), core),
            device_id_type=MESH,
        )

    def part_arrives(d):
        return pltpu.make_async_remote_copy(
            src_ref=ret.at[d - 1],
            dst_ref=part.at[d - 1],
            send_sem=ret_send.at[d - 1],
            recv_sem=part_recv.at[d - 1],
            device_id=at(target(d), core),
            device_id_type=MESH,
        )

    for b, d in steps:
        @pl.when(inside(source(d)) & needed(d, b))
        def _():
            row_copy(d, b).wait_recv()
            span = pl.ds(b * BLOCK, BLOCK)
            their = source(d) * blk_chip + core * blk_dev + b
            whole = slab[...].reshape(n_pair * rows, width)
            t = terms(rx[d - 1, span, :], whole) * same(their, chip_blocks)
            down = jnp.sum(t, axis=0, keepdims=True)
            for c in range(n_pair):
                acc[c] += down[:, c * rows:(c + 1) * rows]
            fold = sum(t[:, j * BLOCK:(j + 1) * BLOCK] for j in range(blk_chip))
            ret[d - 1, :, span] = jnp.sum(fold.T, axis=0, keepdims=True)

        if b == blk_dev - 1:
            @pl.when(inside(source(d)))
            def _():
                return_copy(d).start()

    mate_part = pltpu.make_async_remote_copy(
        src_ref=acc.at[mate],
        dst_ref=part.at[n_sub],
        send_sem=ret_send.at[n_sub],
        recv_sem=part_recv.at[n_sub],
        device_id=at(chip, mate),
        device_id_type=MESH,
    )
    mate_part.start()
    density = density + acc[core]
    mate_part.wait_recv()
    for d in range(1, n_sub + 1):
        @pl.when(inside(target(d)))
        def _():
            part_arrives(d).wait_recv()
    for d in range(n_sub + 1):
        density = density + part[d]
    dens_ref[...] = density

    weight = 1.0 / density
    lane = lax.broadcasted_iota(jnp.int32, (1, rows), 1)
    hi = weight.astype(jnp.bfloat16).astype(jnp.float32)
    mid = (weight - hi).astype(jnp.bfloat16).astype(jnp.float32)
    low = weight - hi - mid
    left = jnp.concatenate(
        [
            jnp.where(lane // BLOCK == b, piece, 0.0)
            for piece in (hi, mid, low)
            for b in range(blk_dev)
        ],
        axis=0,
    ).astype(jnp.bfloat16)
    sums = jnp.dot(left, own, preferred_element_type=jnp.float32)
    sums = (
        sums[0:blk_dev] + sums[blk_dev:2 * blk_dev] + sums[2 * blk_dev:3 * blk_dev]
    )
    totals = jnp.concatenate(
        [
            jnp.sum(weight[:, b * BLOCK:(b + 1) * BLOCK], axis=1, keepdims=True)
            for b in range(blk_dev)
        ],
        axis=0,
    )
    for s in range(n_sub):
        msg[s, :, pl.ds(0, lanes)] = sums[:, lows[s]:lows[s] + lanes]
        msg[s, :, pl.ds(lanes, 128)] = jnp.broadcast_to(totals, (blk_dev, 128))

    def spread(step, carry):
        other = lax.rem(me + step, count)
        other_chip = other // n_pair
        pltpu.make_async_remote_copy(
            src_ref=msg.at[other_chip % n_sub],
            dst_ref=gathered.at[me],
            send_sem=msg_send,
            recv_sem=msg_recv,
            device_id=at(other_chip, other % n_pair),
            device_id_type=MESH,
        ).start()
        return carry

    lax.fori_loop(1, count, spread, 0)
    gathered[me] = msg[sub]

    mate_copy.wait_send()
    mate_part.wait_send()
    for b, d in steps:
        @pl.when(inside(target(d)) & needed(d, b))
        def _():
            row_copy(d, b).wait_send()
    for d in range(1, n_sub + 1):
        @pl.when(inside(source(d)))
        def _():
            return_copy(d).wait_send()

    most = gathered.at[pl.ds(0, count - 1)]
    pltpu.make_async_copy(most, most, msg_recv).wait()

    slot_row = lax.broadcasted_iota(jnp.int32, (8, 1), 0) + run * slots

    def place(q, total):
        got = gathered[q]
        for b in range(blk_dev):
            slot = owner_ref[ids_ref[q * blk_dev + b]]
            total = total + jnp.where(slot_row == slot, got[b:b + 1, :], 0.0)
        return total

    total = lax.fori_loop(
        0, count, place, jnp.zeros((8, lanes + 128), jnp.float32), unroll=4
    )
    proto_ref[...] = (total[:, 0:lanes] / total[:, lanes:lanes + 1])[0:slots]
    pltpu.make_async_copy(most, most, msg_send).wait()


def per_device(sizes, embeddings, block_cluster, owner):
    n_runs, n_sub, n_pair, blk_dev, lows, lanes, slots = sizes
    rows, width = embeddings.shape
    count = n_runs * n_sub * n_pair
    vmem = pl.BlockSpec(memory_space=pltpu.VMEM)
    smem = pl.BlockSpec(memory_space=pltpu.SMEM)
    density, wide = pl.pallas_call(
        functools.partial(kernel, sizes),
        out_shape=(
            jax.ShapeDtypeStruct((1, rows), jnp.float32),
            jax.ShapeDtypeStruct((slots, lanes), jnp.float32),
        ),
        in_specs=[vmem, smem, smem],
        out_specs=(vmem, vmem),
        scratch_shapes=[
            pltpu.VMEM((n_pair, rows, width), jnp.bfloat16),
            pltpu.VMEM((n_sub, rows, width), jnp.bfloat16),
            pltpu.VMEM((n_pair, 1, rows), jnp.float32),
            pltpu.VMEM((n_sub, 1, rows), jnp.float32),
            pltpu.VMEM((n_sub + 1, 1, rows), jnp.float32),
            pltpu.VMEM((n_sub, blk_dev, lanes + 128), jnp.float32),
            pltpu.VMEM((count, blk_dev, lanes + 128), jnp.float32),
            pltpu.SemaphoreType.DMA,
            pltpu.SemaphoreType.DMA,
            pltpu.SemaphoreType.DMA((n_sub, blk_dev)),
            pltpu.SemaphoreType.DMA((n_sub, blk_dev)),
            pltpu.SemaphoreType.DMA((n_sub + 1,)),
            pltpu.SemaphoreType.DMA((n_sub + 1,)),
            pltpu.SemaphoreType.DMA,
            pltpu.SemaphoreType.DMA,
        ],
        compiler_params=pltpu.CompilerParams(
            collective_id=0, has_side_effects=True, vmem_limit_bytes=32 * 1024 * 1024
        ),
    )(embeddings, block_cluster, owner)
    sub = lax.axis_index("sub")
    feature_width = width // n_sub
    offset = sub * feature_width - jnp.asarray(lows, jnp.int32)[sub]
    return (density.reshape(rows), lax.dynamic_slice_in_dim(wide, offset, feature_width, 1))


def solution(mesh):
    placed = (P(("groups", "runs", "sub", "pair"), None), P("groups"), P("groups"))

    def whole(embeddings, block_cluster, owner):
        n_runs, n_sub, n_pair = (mesh.shape[a] for a in ("runs", "sub", "pair"))
        groups = mesh.shape["groups"]
        rows = embeddings.shape[0] // mesh.size
        width = embeddings.shape[1]
        feature_width = width // n_sub
        spans = [
            (s * feature_width // 128 * 128, -(-((s + 1) * feature_width) // 128) * 128)
            for s in range(n_sub)
        ]
        lanes = max(hi - lo for lo, hi in spans)
        lows = tuple(min(lo, width - lanes) for lo, _ in spans)
        slots = owner.shape[0] // groups // n_runs
        sizes = (n_runs, n_sub, n_pair, rows // BLOCK, lows, lanes, slots)
        return jax.shard_map(
            functools.partial(per_device, sizes),
            mesh=mesh,
            in_specs=placed,
            out_specs=(P(("groups", "runs", "sub", "pair")), P(("groups", "runs"), "sub")),
            check_vma=False,
        )(embeddings, block_cluster, owner)

    return whole
```

time: 153 us -> 33 us (0.22)
  waiting for transfers between devices: 93.9 us -> 0 us
  Pallas kernels: 0 us -> 29.2 us
  blocking collectives: 22.6 us -> 0 us
  between operations: 14.8 us -> 0.67 us
  matrix products: 8.21 us -> 0 us
  starting transfers between devices: 6.06 us -> 0 us
  other arithmetic: 4.89 us -> 0 us
    ppermute x2 -> x0, waiting for transfers between devices: 44.8 us -> none  [from_behind(): lax.ppermute(value, axis, [(source, source + steps) for source in range(i...]
    pallas_call x0 -> x1, Pallas kernels: none -> 29.2 us  [per_device(): pl.pallas_call(functools.partial(kernel, sizes), out_shape=(jax.ShapeDtyp...]
    all_gather x1 -> x0, waiting for transfers between devices: 26.9 us -> none  [per_device(): slab = lax.all_gather(unit, ('sub', 'pair'), axis=0, tiled=True)]
    unnamed x3 -> x0, waiting for transfers between devices: 22.2 us -> none
    unnamed x1 -> x0, blocking collectives: 12.4 us -> none
    psum x1 -> x0, blocking collectives: 10.2 us -> none  [per_device(): total, weight_total = lax.psum((slot_sum, slot_weight), ('sub', 'pair'))]
    dot_general x6 -> x0, matrix products: 8.21 us -> none  [the longest x3 6.74 us: tile_terms(): jnp.einsum('ie,je->ij', left, right, preferred_element_type=jnp.float32)]
    ppermute x2 -> x0, starting transfers between devices: 5.98 us -> none  [from_behind(): lax.ppermute(value, axis, [(source, source + steps) for source in range(i...]
  transfers between devices with their start and end apart: 4 -> 0, of which waited for: 3 -> 0; matrix products, arithmetic and copies ran while one was open for 5% -> 0% of each run, Pallas kernels for 0% -> 0%
where the time goes in v1:
time: 33 us; the launch traced here: 32.8 us
  Pallas kernels  29.2 us (88%)
  local copies, waits for them, and re-layouts  2.96 us (9%)
  between operations  0.67 us (2%)
    pallas_call x1, Pallas kernels, per_device(): pl.pallas_call(functools.partial(kernel, sizes), out_shape=(jax.ShapeDtyp...  29.2 us
    unnamed x7, local copies, waits for them, and re-layouts  2.28 us
    dynamic_slice x1, local copies, waits for them, and re-layouts, per_device(): lax.dynamic_slice_in_dim(wide, offset, feature_width, 1)  0.68 us

profile of v1, /device:TPU:0, one launch (start us, length us, event | category | flops | bytes accessed | tf_op | source)
XLA Modules:
  0.0 32.8 jit_solution(3890493957050238910)
XLA Ops:
  0.6 0.0 copy-start.1
  0.6 0.0 copy-start.2
  0.7 0.6 %copy-done.1 = s32[32]{0:T(128)S(1)} copy-done((s32[32]{0:T(128)S(1)}, s32[32]{0:T(128)}, u32[]{:S(2)}) %copy-start.1) | copy-done | bytes 152
  1.3 0.0 copy-done.2
  1.3 0.0 copy-start
  1.3 1.1 %copy-done = bf16[256,1152]{1,0:T(8,128)(2,1)S(1)} copy-done((bf16[256,1152]{1,0:T(8,128)(2,1)S(1)}, bf16[256,1152]{1,0:T(8,128)(2,1)}, u32[]{:S(2)}) %copy-start) | copy-done | bytes 589848
  2.4 29.2 %shard_map.59 = (f32[1,256]{1,0:T(1,128)S(1)}, f32[4,640]{1,0:T(4,128)S(1)}) custom-call(bf16[256,1152]{1,0:T(8,128)(2,1)S(1)} %copy-done, s32[32]{0:T(128)S(1)} %copy-done.1, s32[16]{0:T(128)S(1)} %copy-done.2), custom_call_target="tpu_custom_call" | custom-call | tf_op jit(solution)/shard_map/pallas_call | solution.py:289
  31.5 0.7 %constant_dynamic-slice_fusion = f32[4,576]{1,0:T(4,128)} fusion(f32[4,640]{1,0:T(4,128)S(1)} %get-tuple-element.5, s32[]{:T(128)S(6)} %select_n.7), kind=kLoop, calls=%fused_computation | loop fusion | bytes 18436 | tf_op jit(solution)/shard_map/dynamic_slice | solution.py:321
  32.2 0.6 %copy.7 = f32[256]{0:T(256)} copy(f32[256]{0:T(256)S(1)} %bitcast.1) | data formatting | bytes 2048
Async XLA Ops:
  0.6 0.7 %copy-start.1 = (s32[32]{0:T(128)S(1)}, s32[32]{0:T(128)}, u32[]{:S(2)}) copy-start(s32[32]{0:T(128)} %ids_ref.1) | copy-start | bytes 388
  0.6 0.7 %copy-start.2 = (s32[16]{0:T(128)S(1)}, s32[16]{0:T(128)}, u32[]{:S(2)}) copy-start(s32[16]{0:T(128)} %owner_ref.1) | copy-start | bytes 196
  1.3 1.1 %copy-start = (bf16[256,1152]{1,0:T(8,128)(2,1)S(1)}, bf16[256,1152]{1,0:T(8,128)(2,1)}, u32[]{:S(2)}) copy-start(bf16[256,1152]{1,0:T(8,128)(2,1)} %x_ref.1) | copy-start | bytes 1769476

commit v2 on v1

--- a/solution.py
+++ b/solution.py
@@ -14,11 +14,14 @@
 
 def kernel(
     sizes,
+    x_hbm,
+    ids_hbm,
+    owner_hbm,
+    dens_ref,
+    proto_ref,
     x_ref,
     ids_ref,
     owner_ref,
-    dens_ref,
-    proto_ref,
     slab,
     rx,
     acc,
@@ -26,6 +29,8 @@
     part,
     msg,
     gathered,
+    load_sem,
+    near,
     mate_send,
     mate_recv,
     rows_send,
@@ -36,7 +41,7 @@
     msg_recv,
 ):
     n_runs, n_sub, n_pair, blk_dev, lows, lanes, slots = sizes
-    rows, width = x_ref.shape
+    rows, width = x_hbm.shape
     chips = n_runs * n_sub
     count = chips * n_pair
     blk_chip = blk_dev * n_pair
@@ -52,37 +57,55 @@
             "pair": device_core,
         }
 
+    loads = [
+        pltpu.make_async_copy(
+            x_hbm.at[pl.ds(b * BLOCK, BLOCK)],
+            x_ref.at[pl.ds(b * BLOCK, BLOCK)],
+            load_sem.at[b],
+        )
+        for b in range(blk_dev)
+    ]
+    loads.append(pltpu.make_async_copy(ids_hbm, ids_ref, load_sem.at[blk_dev]))
+    loads.append(pltpu.make_async_copy(owner_hbm, owner_ref, load_sem.at[blk_dev + 1]))
+
     part[...] = jnp.zeros_like(part)
+
+    barrier = pltpu.get_barrier_semaphore()
+    away = [d for step in range(1, n_sub + 1) for d in (step, -step)]
+
+    def inside(c):
+        return (c >= 0) & (c < chips)
+
+    def greet(semaphore):
+        pl.semaphore_signal(semaphore, inc=1, device_id=at(chip, mate), device_id_type=MESH)
+        for d in away:
+            @pl.when(inside(chip + d))
+            def _():
+                pl.semaphore_signal(
+                    semaphore, inc=1, device_id=at(chip + d, core), device_id_type=MESH
+                )
+
+    known = 1 + sum(jnp.where(inside(chip + d), 1, 0) for d in away)
+    greet(barrier)
+    for load in loads:
+        load.start()
     acc[...] = jnp.zeros_like(acc)
     ret[...] = jnp.zeros_like(ret)
 
-    barrier = pltpu.get_barrier_semaphore()
-
-    def greet(step, carry):
-        other = lax.rem(me + step, count)
-        pl.semaphore_signal(
-            barrier, inc=1, device_id=at(other // n_pair, other % n_pair), device_id_type=MESH
-        )
-        return carry
-
-    lax.fori_loop(1, count, greet, 0)
-
     for b in range(blk_dev):
         span = pl.ds(b * BLOCK, BLOCK)
+        loads[b].wait()
         values = x_ref[span, :].astype(jnp.float32)
         mean = jnp.sum(values * values, axis=1, keepdims=True) / width
         slab[core, span, :] = (values * lax.rsqrt(mean + 1e-06)).astype(jnp.bfloat16)
 
-    pl.semaphore_wait(barrier, count - 1)
+    pl.semaphore_wait(barrier, known)
 
     def target(d):
         return chip + d if d < n_sub else chip - n_sub
 
     def source(d):
         return chip - d if d < n_sub else chip + n_sub
-
-    def inside(c):
-        return (c >= 0) & (c < chips)
 
     def needed(d, b):
         return (core * blk_dev + b < blk_chip - 1) if d == n_sub else True
@@ -113,6 +136,8 @@
         device_id_type=MESH,
     )
     mate_copy.start()
+    loads[blk_dev].wait()
+    loads[blk_dev + 1].wait()
     mate_arrives = pltpu.make_async_remote_copy(
         src_ref=slab.at[core],
         dst_ref=slab.at[mate],
@@ -141,12 +166,19 @@
     own_blocks = [me * blk_dev + b for b in range(blk_dev)]
     chip_blocks = [chip * blk_chip + b for b in range(blk_chip)]
 
+    def hop(step, carry):
+        greet(near.at[step])
+        pl.semaphore_wait(near.at[step], known)
+        return carry
+
     density = jnp.zeros((1, rows), jnp.float32)
     own = slab[core]
     for j in range(blk_chip):
         c, b = divmod(j, blk_dev)
         t = terms(slab[c, pl.ds(b * BLOCK, BLOCK), :], own)
         density = density + jnp.sum(t, axis=0, keepdims=True) * same(chip_blocks[j], own_blocks)
+
+    lax.fori_loop(0, near.shape[0], hop, 0)
 
     def return_copy(d):
         return pltpu.make_async_remote_copy(
@@ -285,16 +317,19 @@
     rows, width = embeddings.shape
     count = n_runs * n_sub * n_pair
     vmem = pl.BlockSpec(memory_space=pltpu.VMEM)
-    smem = pl.BlockSpec(memory_space=pltpu.SMEM)
+    hops = -(-(n_runs * n_sub - 1) // n_sub)
     density, wide = pl.pallas_call(
         functools.partial(kernel, sizes),
         out_shape=(
             jax.ShapeDtypeStruct((1, rows), jnp.float32),
             jax.ShapeDtypeStruct((slots, lanes), jnp.float32),
         ),
-        in_specs=[vmem, smem, smem],
+        in_specs=[pl.BlockSpec(memory_space=pl.ANY)] * 3,
         out_specs=(vmem, vmem),
         scratch_shapes=[
+            pltpu.VMEM((rows, width), jnp.bfloat16),
+            pltpu.SMEM(block_cluster.shape, jnp.int32),
+            pltpu.SMEM(owner.shape, jnp.int32),
             pltpu.VMEM((n_pair, rows, width), jnp.bfloat16),
             pltpu.VMEM((n_sub, rows, width), jnp.bfloat16),
             pltpu.VMEM((n_pair, 1, rows), jnp.float32),
@@ -302,6 +337,8 @@
             pltpu.VMEM((n_sub + 1, 1, rows), jnp.float32),
             pltpu.VMEM((n_sub, blk_dev, lanes + 128), jnp.float32),
             pltpu.VMEM((count, blk_dev, lanes + 128), jnp.float32),
+            pltpu.SemaphoreType.DMA((blk_dev + 2,)),
+            pltpu.SemaphoreType.REGULAR((hops,)),
             pltpu.SemaphoreType.DMA,
             pltpu.SemaphoreType.DMA,
             pltpu.SemaphoreType.DMA((n_sub, blk_dev)),

time: 33 us -> 31 us (0.939)
  Pallas kernels: 29.2 us -> 27.2 us
    pallas_call x1, Pallas kernels: 29.2 us -> 27.2 us  [per_device(): pl.pallas_call(functools.partial(kernel, sizes), out_shape=(jax.ShapeDtyp...]
where the time goes in v2:
time: 31 us; the launch traced here: 30.8 us
  Pallas kernels  27.2 us (88%)
  local copies, waits for them, and re-layouts  2.96 us (10%)
  between operations  0.67 us (2%)
    pallas_call x1, Pallas kernels, per_device(): pl.pallas_call(functools.partial(kernel, sizes), out_shape=(jax.ShapeDtyp...  27.2 us
    unnamed x7, local copies, waits for them, and re-layouts  2.28 us
    dynamic_slice x1, local copies, waits for them, and re-layouts, per_device(): lax.dynamic_slice_in_dim(wide, offset, feature_width, 1)  0.68 us

profile of v2, /device:TPU:0, one launch (start us, length us, event | category | flops | bytes accessed | tf_op | source)
XLA Modules:
  0.0 30.8 jit_solution(8142958302130354301)
XLA Ops:
  0.6 0.0 copy-start.1
  0.6 0.0 copy-start.2
  0.7 0.6 %copy-done.1 = s32[32]{0:T(128)S(1)} copy-done((s32[32]{0:T(128)S(1)}, s32[32]{0:T(128)}, u32[]{:S(2)}) %copy-start.1) | copy-done | bytes 152
  1.3 0.0 copy-done.2
  1.3 0.0 copy-start
  1.3 1.1 %copy-done = bf16[256,1152]{1,0:T(8,128)(2,1)S(1)} copy-done((bf16[256,1152]{1,0:T(8,128)(2,1)S(1)}, bf16[256,1152]{1,0:T(8,128)(2,1)}, u32[]{:S(2)}) %copy-start) | copy-done | bytes 589848
  2.4 27.2 %shard_map.59 = (f32[1,256]{1,0:T(1,128)S(1)}, f32[4,640]{1,0:T(4,128)S(1)}) custom-call(bf16[256,1152]{1,0:T(8,128)(2,1)S(1)} %copy-done, s32[32]{0:T(128)S(1)} %copy-done.1, s32[16]{0:T(128)S(1)} %copy-done.2), custom_call_target="tpu_custom_call" | custom-call | tf_op jit(solution)/shard_map/pallas_call | solution.py:321
  29.6 0.7 %constant_dynamic-slice_fusion = f32[4,576]{1,0:T(4,128)} fusion(f32[4,640]{1,0:T(4,128)S(1)} %get-tuple-element.5, s32[]{:T(128)S(6)} %select_n.7), kind=kLoop, calls=%fused_computation | loop fusion | bytes 18436 | tf_op jit(solution)/shard_map/dynamic_slice | solution.py:358
  30.2 0.6 %copy.7 = f32[256]{0:T(256)} copy(f32[256]{0:T(256)S(1)} %bitcast.1) | data formatting | bytes 2048
Async XLA Ops:
  0.6 0.7 %copy-start.1 = (s32[32]{0:T(128)S(1)}, s32[32]{0:T(128)}, u32[]{:S(2)}) copy-start(s32[32]{0:T(128)} %ids_hbm.1) | copy-start | bytes 388
  0.6 0.7 %copy-start.2 = (s32[16]{0:T(128)S(1)}, s32[16]{0:T(128)}, u32[]{:S(2)}) copy-start(s32[16]{0:T(128)} %owner_hbm.1) | copy-start | bytes 196
  1.3 1.1 %copy-start = (bf16[256,1152]{1,0:T(8,128)(2,1)S(1)}, bf16[256,1152]{1,0:T(8,128)(2,1)}, u32[]{:S(2)}) copy-start(bf16[256,1152]{1,0:T(8,128)(2,1)} %x_hbm.1) | copy-start | bytes 1769476

commit v3 on v2

--- a/solution.py
+++ b/solution.py
@@ -42,6 +42,7 @@
 ):
     n_runs, n_sub, n_pair, blk_dev, lows, lanes, slots = sizes
     rows, width = x_hbm.shape
+    feature_width = width // n_sub
     chips = n_runs * n_sub
     count = chips * n_pair
     blk_chip = blk_dev * n_pair
@@ -89,17 +90,6 @@
     greet(barrier)
     for load in loads:
         load.start()
-    acc[...] = jnp.zeros_like(acc)
-    ret[...] = jnp.zeros_like(ret)
-
-    for b in range(blk_dev):
-        span = pl.ds(b * BLOCK, BLOCK)
-        loads[b].wait()
-        values = x_ref[span, :].astype(jnp.float32)
-        mean = jnp.sum(values * values, axis=1, keepdims=True) / width
-        slab[core, span, :] = (values * lax.rsqrt(mean + 1e-06)).astype(jnp.bfloat16)
-
-    pl.semaphore_wait(barrier, known)
 
     def target(d):
         return chip + d if d < n_sub else chip - n_sub
@@ -113,7 +103,7 @@
     def row_copy(d, b):
         span = pl.ds(b * BLOCK, BLOCK)
         return pltpu.make_async_remote_copy(
-            src_ref=slab.at[core, span, :],
+            src_ref=x_hbm.at[span, :],
             dst_ref=rx.at[d - 1, span, :],
             send_sem=rows_send.at[d - 1, b],
             recv_sem=rows_recv.at[d - 1, b],
@@ -121,11 +111,25 @@
             device_id_type=MESH,
         )
 
-    steps = [(b, d) for b in range(blk_dev) for d in range(1, n_sub + 1)]
-    for b, d in steps:
+    starts = [(b, d) for d in range(1, n_sub + 1) for b in range(blk_dev)]
+    steps = [(b, d) for b in range(blk_dev) for d in range(n_sub, 0, -1)]
+    pl.semaphore_wait(barrier, known)
+    for b, d in starts:
         @pl.when(inside(target(d)) & needed(d, b))
         def _():
             row_copy(d, b).start()
+
+    def normal(values):
+        values = values.astype(jnp.float32)
+        mean = jnp.sum(values * values, axis=1, keepdims=True) / width
+        return (values * lax.rsqrt(mean + 1e-06)).astype(jnp.bfloat16)
+
+    acc[...] = jnp.zeros_like(acc)
+    ret[...] = jnp.zeros_like(ret)
+    for b in range(blk_dev):
+        span = pl.ds(b * BLOCK, BLOCK)
+        loads[b].wait()
+        slab[core, span, :] = normal(x_ref[span, :])
 
     mate_copy = pltpu.make_async_remote_copy(
         src_ref=slab.at[core],
@@ -207,7 +211,7 @@
             span = pl.ds(b * BLOCK, BLOCK)
             their = source(d) * blk_chip + core * blk_dev + b
             whole = slab[...].reshape(n_pair * rows, width)
-            t = terms(rx[d - 1, span, :], whole) * same(their, chip_blocks)
+            t = terms(normal(rx[d - 1, span, :]), whole) * same(their, chip_blocks)
             down = jnp.sum(t, axis=0, keepdims=True)
             for c in range(n_pair):
                 acc[c] += down[:, c * rows:(c + 1) * rows]
@@ -263,23 +267,29 @@
         axis=0,
     )
     for s in range(n_sub):
-        msg[s, :, pl.ds(0, lanes)] = sums[:, lows[s]:lows[s] + lanes]
-        msg[s, :, pl.ds(lanes, 128)] = jnp.broadcast_to(totals, (blk_dev, 128))
-
-    def spread(step, carry):
-        other = lax.rem(me + step, count)
-        other_chip = other // n_pair
-        pltpu.make_async_remote_copy(
-            src_ref=msg.at[other_chip % n_sub],
-            dst_ref=gathered.at[me],
-            send_sem=msg_send,
-            recv_sem=msg_recv,
-            device_id=at(other_chip, other % n_pair),
-            device_id_type=MESH,
-        ).start()
+        column = lax.broadcasted_iota(jnp.int32, (blk_dev, lanes), 1) + (lows[s] - s * feature_width)
+        mine = (column >= 0) & (column < feature_width)
+        msg[s] = jnp.where(mine, sums[:, lows[s]:lows[s] + lanes], totals)
+
+    def spread(far, carry):
+        to_run = lax.rem(run + far, n_runs)
+        for x in range(n_sub):
+            to_sub = lax.rem(sub + x, n_sub)
+            for c in range(n_pair):
+                if isinstance(far, int) and x + c == 0:
+                    continue
+                pltpu.make_async_remote_copy(
+                    src_ref=msg.at[to_sub],
+                    dst_ref=gathered.at[me],
+                    send_sem=msg_send,
+                    recv_sem=msg_recv,
+                    device_id={"runs": to_run, "sub": to_sub, "pair": lax.rem(core + c, n_pair)},
+                    device_id_type=MESH,
+                ).start()
         return carry
 
-    lax.fori_loop(1, count, spread, 0)
+    lax.fori_loop(1, n_runs, spread, 0, unroll=min(3, n_runs - 1))
+    spread(0, 0)
     gathered[me] = msg[sub]
 
     mate_copy.wait_send()
@@ -306,9 +316,10 @@
         return total
 
     total = lax.fori_loop(
-        0, count, place, jnp.zeros((8, lanes + 128), jnp.float32), unroll=4
-    )
-    proto_ref[...] = (total[:, 0:lanes] / total[:, lanes:lanes + 1])[0:slots]
+        0, count, place, jnp.zeros((8, lanes), jnp.float32), unroll=8
+    )
+    weights = jnp.where(sub == 0, total[:, feature_width:feature_width + 1], total[:, 0:1])
+    proto_ref[...] = (total / weights)[0:slots]
     pltpu.make_async_copy(most, most, msg_send).wait()
 
 
@@ -335,8 +346,8 @@
             pltpu.VMEM((n_pair, 1, rows), jnp.float32),
             pltpu.VMEM((n_sub, 1, rows), jnp.float32),
             pltpu.VMEM((n_sub + 1, 1, rows), jnp.float32),
-            pltpu.VMEM((n_sub, blk_dev, lanes + 128), jnp.float32),
-            pltpu.VMEM((count, blk_dev, lanes + 128), jnp.float32),
+            pltpu.VMEM((n_sub, blk_dev, lanes), jnp.float32),
+            pltpu.VMEM((count, blk_dev, lanes), jnp.float32),
             pltpu.SemaphoreType.DMA((blk_dev + 2,)),
             pltpu.SemaphoreType.REGULAR((hops,)),
             pltpu.SemaphoreType.DMA,
@@ -372,6 +383,7 @@
             for s in range(n_sub)
         ]
         lanes = max(hi - lo for lo, hi in spans)
+        assert lanes > feature_width, feature_width
         lows = tuple(min(lo, width - lanes) for lo, _ in spans)
         slots = owner.shape[0] // groups // n_runs
         sizes = (n_runs, n_sub, n_pair, rows // BLOCK, lows, lanes, slots)

time: 31 us -> 30.9 us (level)
  no operation moved by 1% of the time
where the time goes in v3:
time: 30.9 us; the launch traced here: 30.7 us
  Pallas kernels  27.1 us (88%)
  local copies, waits for them, and re-layouts  2.96 us (10%)
  between operations  0.67 us (2%)
    pallas_call x1, Pallas kernels, per_device(): pl.pallas_call(functools.partial(kernel, sizes), out_shape=(jax.ShapeDtyp...  27.1 us
    unnamed x7, local copies, waits for them, and re-layouts  2.28 us
    dynamic_slice x1, local copies, waits for them, and re-layouts, per_device(): lax.dynamic_slice_in_dim(wide, offset, feature_width, 1)  0.68 us

profile of v3, /device:TPU:0, one launch (start us, length us, event | category | flops | bytes accessed | tf_op | source)
XLA Modules:
  0.0 30.7 jit_solution(13063225019658151814)
XLA Ops:
  0.6 0.0 copy-start.1
  0.6 0.0 copy-start.2
  0.7 0.6 %copy-done.1 = s32[32]{0:T(128)S(1)} copy-done((s32[32]{0:T(128)S(1)}, s32[32]{0:T(128)}, u32[]{:S(2)}) %copy-start.1) | copy-done | bytes 152
  1.3 0.0 copy-done.2
  1.3 0.0 copy-start
  1.3 1.1 %copy-done = bf16[256,1152]{1,0:T(8,128)(2,1)S(1)} copy-done((bf16[256,1152]{1,0:T(8,128)(2,1)S(1)}, bf16[256,1152]{1,0:T(8,128)(2,1)}, u32[]{:S(2)}) %copy-start) | copy-done | bytes 589848
  2.4 27.1 %shard_map.59 = (f32[1,256]{1,0:T(1,128)S(1)}, f32[4,640]{1,0:T(4,128)S(1)}) custom-call(bf16[256,1152]{1,0:T(8,128)(2,1)S(1)} %copy-done, s32[32]{0:T(128)S(1)} %copy-done.1, s32[16]{0:T(128)S(1)} %copy-done.2), custom_call_target="tpu_custom_call" | custom-call | tf_op jit(solution)/shard_map/pallas_call | solution.py:332
  29.5 0.7 %constant_dynamic-slice_fusion = f32[4,576]{1,0:T(4,128)} fusion(f32[4,640]{1,0:T(4,128)S(1)} %get-tuple-element.5, s32[]{:T(128)S(6)} %select_n.7), kind=kLoop, calls=%fused_computation | loop fusion | bytes 18436 | tf_op jit(solution)/shard_map/dynamic_slice | solution.py:369
  30.2 0.6 %copy.7 = f32[256]{0:T(256)} copy(f32[256]{0:T(256)S(1)} %bitcast.1) | data formatting | bytes 2048
Async XLA Ops:
  0.6 0.7 %copy-start.1 = (s32[32]{0:T(128)S(1)}, s32[32]{0:T(128)}, u32[]{:S(2)}) copy-start(s32[32]{0:T(128)} %ids_hbm.1) | copy-start | bytes 388
  0.6 0.7 %copy-start.2 = (s32[16]{0:T(128)S(1)}, s32[16]{0:T(128)}, u32[]{:S(2)}) copy-start(s32[16]{0:T(128)} %owner_hbm.1) | copy-start | bytes 196
  1.3 1.1 %copy-start = (bf16[256,1152]{1,0:T(8,128)(2,1)S(1)}, bf16[256,1152]{1,0:T(8,128)(2,1)}, u32[]{:S(2)}) copy-start(bf16[256,1152]{1,0:T(8,128)(2,1)} %x_hbm.1) | copy-start | bytes 1769476
